TPU v7x, 128 devices: a whole 4x4x4 slice. The times are simulated.
128 devices in a mesh: section: 8 (over z, y_hi), dp: 16 (over y_lo, x, core).
Axes of the slice: x: 4, y: 4 (y_hi: 2, y_lo: 2; y = y_hi * 2 + y_lo), z: 4, core: 2. Of those that a mesh axis runs over, the one named last changes fastest.
Arguments:
- inputs: bfloat16 [4, 768, 4096], P(None, 'dp'), may hold values from -6 to 6
- cotangent: bfloat16 [4, 768, 4096], P(None, 'dp'), may hold values from -0.119628906 to 0.119628906
- w_in: bfloat16 [2, 8, 4096, 256], P(None, 'section', 'dp'), may hold values from -0.09375 to 0.09375
- w_out: bfloat16 [2, 8, 4096, 256], P(None, 'section', 'dp'), may hold values from -0.375 to 0.375
- norm_gain: bfloat16 [2, 8, 4096], P(None, 'section', 'dp'), may hold values from 0.5 to 1.5
Outputs:
- w_in_grad: float32 [2, 8, 4096, 256], P(None, 'section', 'dp')
- w_out_grad: float32 [2, 8, 4096, 256], P(None, 'section', 'dp')
- gain_grad: float32 [2, 8, 4096], P(None, 'section', 'dp')
All inputs are finite; a program needn't handle non-finite values.
Results may differ from a plain program's by a relative error of at most 0.04.
Values may be sent and summed in bfloat16 or wider, within the bound.
No kernel may reach another device: no remote copies, remote signals or barrier semaphores. Data moves between devices by JAX's collectives and lax.ppermute only.
A program may use at most 128 MiB of HBM per device.

v0:
```python
import jax
import jax.numpy as jnp
from jax import lax
from jax.sharding import PartitionSpec as P

EPS = 1e-06


def from_behind(value, axis, steps):
    count = lax.axis_size(axis)
    first, last = (max(0, -steps), min(count, count - steps))
    return lax.ppermute(value, axis, [(source, source + steps) for source in range(first, last)])


def norm_parts(layer_input, norm_gain, w_in):
    widened = layer_input.astype(jnp.float32)
    inv_rms = lax.rsqrt(jnp.mean(widened * widened, axis=-1, keepdims=True) + EPS)
    normed = (widened * inv_rms * norm_gain.astype(jnp.float32)).astype(jnp.bfloat16)
    active = jnp.dot(normed, w_in, preferred_element_type=jnp.float32)
    return (widened, inv_rms, normed, active)


def layer_forward(layer_input, norm_gain, w_in, w_out):
    widened, inv_rms, normed, active = norm_parts(layer_input, norm_gain, w_in)
    lifted = jax.nn.silu(active).astype(jnp.bfloat16)
    branch_out = lax.dot_general(
        lifted, w_out, (((1,), (1,)), ((), ())), preferred_element_type=jnp.float32
    )
    return ((widened + branch_out).astype(jnp.bfloat16), normed, active)


def layer_backward(layer_input, active, norm_gain, w_in, w_out, upstream):
    widened = layer_input.astype(jnp.float32)
    inv_rms = lax.rsqrt(jnp.mean(widened * widened, axis=-1, keepdims=True) + EPS)
    lifted = jax.nn.silu(active).astype(jnp.bfloat16)
    grad_lift = jnp.dot(upstream, w_out, preferred_element_type=jnp.float32)
    logistic = jax.nn.sigmoid(active)
    grad_act = (grad_lift * logistic * (1.0 + active * (1.0 - logistic))).astype(jnp.bfloat16)
    grad_norm = lax.dot_general(
        grad_act, w_in, (((1,), (1,)), ((), ())), preferred_element_type=jnp.float32
    )
    scaled = grad_norm * norm_gain.astype(jnp.float32)
    inner_mean = jnp.mean(widened * scaled, axis=-1, keepdims=True)
    cubed = inv_rms * inv_rms * inv_rms
    grad_input = (
        upstream.astype(jnp.float32) + inv_rms * scaled - widened * cubed * inner_mean
    ).astype(jnp.bfloat16)
    gain_piece = jnp.sum(grad_norm * widened * inv_rms, axis=0)
    return (grad_input, grad_act, lifted, gain_piece)


def fetch_row(buffer, slot_index):
    return lax.dynamic_index_in_dim(buffer, slot_index, 0, keepdims=False)


def per_device(inputs, cotangent, w_in, w_out, norm_gain):
    full_in, full_out, full_gain = (
        lax.all_gather(w_in, "dp", axis=2, tiled=True),
        lax.all_gather(w_out, "dp", axis=2, tiled=True),
        lax.all_gather(norm_gain, "dp", axis=2, tiled=True),
    )
    sections = lax.axis_size("section")
    section_here = lax.axis_index("section")
    batches, tok_rows, features = inputs.shape
    lowrank = w_in.shape[3]
    ticks = sections + batches - 1
    zero_rows = jnp.zeros((tok_rows, features), jnp.bfloat16)
    zero_narrow = jnp.zeros((tok_rows, lowrank), jnp.bfloat16)
    zero_gain = jnp.zeros((features,), jnp.float32)

    def run_phase(feed, layer_step, empty_set, upward):
        position = section_here if upward else sections - 1 - section_here

        def advance(moment, carried):
            incoming, records, totals = carried
            slot_pos = moment - position
            in_range = jnp.logical_and(slot_pos >= 0, slot_pos < batches)
            slot_index = jnp.clip(slot_pos, 0, batches - 1)
            source = jnp.where(position == 0, fetch_row(feed, slot_index), incoming)
            outgoing, new_rows, gain_piece = lax.cond(
                in_range, lambda: layer_step(source, slot_index), lambda: empty_set
            )
            records = tuple(
                (
                    lax.dynamic_update_index_in_dim(
                        buffer,
                        jnp.where(in_range, fresh_row, fetch_row(buffer, slot_index)),
                        slot_index,
                        0,
                    )
                    for buffer, fresh_row in zip(records, new_rows)
                )
            )
            totals = totals + gain_piece
            if upward:
                incoming = from_behind(outgoing, "section", 1)
            else:
                incoming = from_behind(outgoing, "section", -1)
            return (incoming, records, totals)

        initial = (
            zero_rows,
            tuple((jnp.zeros((batches,) + item.shape, item.dtype) for item in empty_set[1])),
            zero_gain,
        )
        finished = lax.fori_loop(0, ticks, advance, initial)
        return (finished[1], finished[2])

    def forward_step(half_index):
        gain_now, in_now, out_now = (
            full_gain[half_index, 0],
            full_in[half_index, 0],
            full_out[half_index, 0],
        )

        def layer_step(source, slot_index):
            result, normed, active = layer_forward(source, gain_now, in_now, out_now)
            return (result, (source, result), zero_gain)

        return layer_step

    def backward_step(half_index, entered):
        gain_now, in_now, out_now = (
            full_gain[half_index, 0],
            full_in[half_index, 0],
            full_out[half_index, 0],
        )

        def layer_step(source, slot_index):
            layer_input = fetch_row(entered, slot_index)
            _, _, normed, active = norm_parts(layer_input, gain_now, in_now)
            grad_input, grad_act, lifted, gain_piece = layer_backward(
                layer_input, active, gain_now, in_now, out_now, source
            )
            return (grad_input, (grad_input, normed, grad_act, lifted, source), gain_piece)

        return layer_step

    forward_empty = (zero_rows, (zero_rows, zero_rows), zero_gain)
    backward_empty = (
        zero_rows,
        (zero_rows, zero_rows, zero_narrow, zero_narrow, zero_rows),
        zero_gain,
    )
    first_fwd, _ = run_phase(inputs, forward_step(0), forward_empty, True)
    second_fwd, _ = run_phase(first_fwd[1], forward_step(1), forward_empty, False)
    second_bwd, second_gain = run_phase(
        cotangent, backward_step(1, second_fwd[0]), backward_empty, True
    )
    first_bwd, first_gain = run_phase(
        second_bwd[0], backward_step(0, first_fwd[0]), backward_empty, False
    )
    every_row = batches * tok_rows
    normeds = jnp.stack([first_bwd[1], second_bwd[1]]).reshape(2, every_row, features)
    grad_acts = jnp.stack([first_bwd[2], second_bwd[2]]).reshape(2, every_row, lowrank)
    liftings = jnp.stack([first_bwd[3], second_bwd[3]]).reshape(2, every_row, lowrank)
    uppers = jnp.stack([first_bwd[4], second_bwd[4]]).reshape(2, every_row, features)
    gain_sums = jnp.stack([first_gain, second_gain])
    in_block = jnp.einsum("lnd,lnk->dlk", normeds, grad_acts, preferred_element_type=jnp.float32)
    out_block = jnp.einsum("lnd,lnk->dlk", uppers, liftings, preferred_element_type=jnp.float32)
    shares = lax.psum_scatter(
        jnp.stack([in_block, out_block], 1).astype(jnp.bfloat16),
        "dp",
        scatter_dimension=0,
        tiled=True,
    ).astype(jnp.float32)
    grad_in_w = jnp.transpose(shares[:, 0], (1, 0, 2))
    grad_out_w = jnp.transpose(shares[:, 1], (1, 0, 2))
    gain_share = lax.psum_scatter(
        gain_sums.astype(jnp.bfloat16), "dp", scatter_dimension=1, tiled=True
    ).astype(jnp.float32)
    return (grad_in_w[:, None], grad_out_w[:, None], gain_share[:, None])


def solution(mesh):
    return jax.shard_map(
        per_device,
        mesh=mesh,
        in_specs=(
            P(None, "dp", None),
            P(None, "dp", None),
            P(None, "section", "dp", None),
            P(None, "section", "dp", None),
            P(None, "section", "dp"),
        ),
        out_specs=(
            P(None, "section", "dp", None),
            P(None, "section", "dp", None),
            P(None, "section", "dp"),
        ),
        check_vma=False,
    )
```

profile of v0, /device:TPU:0, one launch (start us, length us, event | category | flops | bytes accessed | tf_op | source)
XLA Modules:
  0.0 1125.0 jit_solution(7650921075710210025)
XLA Ops:
  8.7 20.0 %all_gather.9 = bf16[2,1,4096]{2,0,1:T(2,128)(2,1)S(1)} all-gather(bf16[2,1,256]{2,0,1:T(2,128)(2,1)} %param.25), channel_id=1, replica_groups=mesh['section'=8,'dp'=16] {'dp'}, dimensions={2}, use_global_device_ids=true | all-gather | bytes 17408 | tf_op jit(solution)/shard_map/all_gather | solution.py:60
  28.9 20.6 %all-gather.5.cloned.1.call-done = bf16[2,1,4096,256]{3,2,1,0:T(8,128)(2,1)} async-done(((bf16[2,1,256,256]{3,2,1,0:T(8,128)(2,1)}), bf16[2,1,4096,256]{3,2,1,0:T(8,128)(2,1)}) %all-gather.5.cloned.1.call-update) | async-done | bytes 4194320 | tf_op jit(solution)/shard_map/all_gather | solution.py:59
  53.9 34.6 %all-gather.3.cloned.1.call-done = bf16[2,1,4096,256]{3,2,1,0:T(8,128)(2,1)} async-done(((bf16[2,1,256,256]{3,2,1,0:T(8,128)(2,1)}), bf16[2,1,4096,256]{3,2,1,0:T(8,128)(2,1)}) %all-gather.3.cloned.1.call-update) | async-done | bytes 4194320 | tf_op jit(solution)/shard_map/all_gather | solution.py:58
  95.1 169.6 %while.86 = (s32[]{:T(128)}, bf16[48,4096]{1,0:T(8,128)(2,1)S(1)}, bf16[4,48,4096]{2,1,0:T(8,128)(2,1)}, bf16[4,48,4096]{2,1,0:T(8,128)(2,1)}, s32[]{:T(128)}, /...) while((s32[]{:T(128)}, bf16[48,4096]{1,0:T(8,128)(2,1)S(1)}, ...), condition=%wide.region_4.5_spmd, body=%wide.region_0.4_spmd.sunk | while | flops 203948096 | bytes 11707969 | solution.py:106
  167.5 10.5 collective-permute-start
  196.3 11.3 %collective-permute-start = (bf16[48,4096]{1,0:T(8,128)(2,1)S(1)}, bf16[48,4096]{1,0:T(8,128)(2,1)S(1)}, u32[]{:S(2)}, u32[]{:S(2)}) collective-permute-start(bf16[48,4096]{1,0:T(8,128)(2,1)S(1)} %get-tuple-element.1734), channel_id=1, source_target_pairs={{0,16},{16,32},{32,48},{48,64},{64,80},{80,96},{96,112},{1,17},{17... | collective-permute-start | bytes 1179656 | tf_op jit(solution)/shard_map/while/body/eval_jaxpr/ppermute | solution.py:12
  266.0 222.8 %while.87 = (s32[]{:T(128)}, bf16[48,4096]{1,0:T(8,128)(2,1)S(1)}, bf16[4,48,4096]{2,1,0:T(8,128)(2,1)}, s32[]{:T(128)}, pred[]{:T(512)}, /*index=5*/bf16[4,48,4...) while((s32[]{:T(128)}, bf16[48,4096]{1,0:T(8,128)(2,1)S(1)}, ...), condition=%wide.region_9.10_spmd, body=%wide.region_5.9_spmd.sunk | while | flops 203751488 | bytes 9741877 | solution.py:106
  270.1 15.1 %collective-permute-done.1 = bf16[48,4096]{1,0:T(8,128)(2,1)S(1)} collective-permute-done((bf16[48,4096]{1,0:T(8,128)(2,1)S(1)}, bf16[48,4096]{1,0:T(8,128)(2,1)S(1)}, u32[]{:S(2)}, u32[]{:S(2)}) %collective-permute-start.1) | collective-permute-done | bytes 393248 | tf_op jit(solution)/shard_map/while/body/eval_jaxpr/ppermute | solution.py:12
  289.3 11.8 %collective-permute-done.1 = bf16[48,4096]{1,0:T(8,128)(2,1)S(1)} collective-permute-done((bf16[48,4096]{1,0:T(8,128)(2,1)S(1)}, bf16[48,4096]{1,0:T(8,128)(2,1)S(1)}, u32[]{:S(2)}, u32[]{:S(2)}) %collective-permute-start.1) | collective-permute-done | bytes 393248 | tf_op jit(solution)/shard_map/while/body/eval_jaxpr/ppermute | solution.py:12
  305.1 12.4 %collective-permute-done.1 = bf16[48,4096]{1,0:T(8,128)(2,1)S(1)} collective-permute-done((bf16[48,4096]{1,0:T(8,128)(2,1)S(1)}, bf16[48,4096]{1,0:T(8,128)(2,1)S(1)}, u32[]{:S(2)}, u32[]{:S(2)}) %collective-permute-start.1) | collective-permute-done | bytes 393248 | tf_op jit(solution)/shard_map/while/body/eval_jaxpr/ppermute | solution.py:12
  321.5 14.1 %collective-permute-done.1 = bf16[48,4096]{1,0:T(8,128)(2,1)S(1)} collective-permute-done((bf16[48,4096]{1,0:T(8,128)(2,1)S(1)}, bf16[48,4096]{1,0:T(8,128)(2,1)S(1)}, u32[]{:S(2)}, u32[]{:S(2)}) %collective-permute-start.1) | collective-permute-done | bytes 393248 | tf_op jit(solution)/shard_map/while/body/eval_jaxpr/ppermute | solution.py:12
  339.6 13.2 %collective-permute-done.1 = bf16[48,4096]{1,0:T(8,128)(2,1)S(1)} collective-permute-done((bf16[48,4096]{1,0:T(8,128)(2,1)S(1)}, bf16[48,4096]{1,0:T(8,128)(2,1)S(1)}, u32[]{:S(2)}, u32[]{:S(2)}) %collective-permute-start.1) | collective-permute-done | bytes 393248 | tf_op jit(solution)/shard_map/while/body/eval_jaxpr/ppermute | solution.py:12
  368.8 45.9 %collective-permute-done.1 = bf16[48,4096]{1,0:T(8,128)(2,1)S(1)} collective-permute-done((bf16[48,4096]{1,0:T(8,128)(2,1)S(1)}, bf16[48,4096]{1,0:T(8,128)(2,1)S(1)}, u32[]{:S(2)}, u32[]{:S(2)}) %collective-permute-start.1) | collective-permute-done | bytes 393248 | tf_op jit(solution)/shard_map/while/body/eval_jaxpr/ppermute | solution.py:12
  424.9 9.8 collective-permute-done.1
  444.9 8.9 collective-permute-done.1
  493.0 212.0 %while.88 = (s32[]{:T(128)}, bf16[48,4096]{1,0:T(8,128)(2,1)S(1)}, bf16[4,48,4096]{2,1,0:T(8,128)(2,1)}, bf16[4,48,4096]{2,1,0:T(8,128)(2,1)}, bf16[4,48,256]{2,...) while((s32[]{:T(128)}, bf16[48,4096]{1,0:T(8,128)(2,1)S(1)}, ...), condition=%wide.region_16.17_spmd.clone, body=%wide.region_10.16_spmd.clone.sunk | while | flops 307503232 | bytes 47157208 | solution.py:106
  493.0 10.5 conditional.12
  512.7 10.5 conditional.12
  536.0 10.5 conditional.12
  559.2 10.5 conditional.12
  582.5 14.1 %collective-permute-start.2 = (bf16[48,4096]{1,0:T(8,128)(2,1)S(1)}, bf16[48,4096]{1,0:T(8,128)(2,1)S(1)}, u32[]{:S(2)}, u32[]{:S(2)}) collective-permute-start(bf16[48,4096]{1,0:T(8,128)(2,1)S(1)} %get-tuple-element.1764), channel_id=1, source_target_pairs={{0,16},{16,32},{32,48},{48,64},{64,80},{80,96},{96,112},{1,17},{17... | collective-permute-start | bytes 1179656 | tf_op jit(solution)/shard_map/while/body/eval_jaxpr/ppermute | solution.py:12
  616.0 17.5 %collective-permute-start.2 = (bf16[48,4096]{1,0:T(8,128)(2,1)S(1)}, bf16[48,4096]{1,0:T(8,128)(2,1)S(1)}, u32[]{:S(2)}, u32[]{:S(2)}) collective-permute-start(bf16[48,4096]{1,0:T(8,128)(2,1)S(1)} %get-tuple-element.1764), channel_id=1, source_target_pairs={{0,16},{16,32},{32,48},{48,64},{64,80},{80,96},{96,112},{1,17},{17... | collective-permute-start | bytes 1179656 | tf_op jit(solution)/shard_map/while/body/eval_jaxpr/ppermute | solution.py:12
  690.6 8.7 collective-permute-start.2
  709.0 269.9 %while.89 = (s32[]{:T(128)}, bf16[48,4096]{1,0:T(8,128)(2,1)S(1)}, bf16[4,48,4096]{2,1,0:T(8,128)(2,1)}, bf16[4,48,256]{2,1,0:T(8,128)(2,1)}, bf16[4,48,256]{2,1...) while((s32[]{:T(128)}, bf16[48,4096]{1,0:T(8,128)(2,1)S(1)}, ...), condition=%wide.region_23.24_spmd.clone, body=%wide.region_17.23_spmd.clone.sunk | while | flops 307306624 | bytes 30510992 | solution.py:106
  789.9 15.0 %collective-permute-done.3 = bf16[48,4096]{1,0:T(8,128)(2,1)S(1)} collective-permute-done((bf16[48,4096]{1,0:T(8,128)(2,1)S(1)}, bf16[48,4096]{1,0:T(8,128)(2,1)S(1)}, u32[]{:S(2)}, u32[]{:S(2)}) %collective-permute-start.3) | collective-permute-done | bytes 393248 | tf_op jit(solution)/shard_map/while/body/eval_jaxpr/ppermute | solution.py:12
  813.0 78.4 %collective-permute-done.3 = bf16[48,4096]{1,0:T(8,128)(2,1)S(1)} collective-permute-done((bf16[48,4096]{1,0:T(8,128)(2,1)S(1)}, bf16[48,4096]{1,0:T(8,128)(2,1)S(1)}, u32[]{:S(2)}, u32[]{:S(2)}) %collective-permute-start.3) | collective-permute-done | bytes 393248 | tf_op jit(solution)/shard_map/while/body/eval_jaxpr/ppermute | solution.py:12
  891.4 9.8 conditional.13
  913.0 9.8 conditional.13
  934.8 9.8 conditional.13
  957.9 9.8 conditional.13
  994.6 45.0 %reduce-scatter.7.cloned.1.call-done = bf16[256,2]{1,0:T(8,128)(2,1)} async-done(((bf16[4096,2]{1,0:T(8,128)(2,1)}), bf16[256,2]{1,0:T(8,128)(2,1)}) %reduce-scatter.7.cloned.1.call-update) | async-done | bytes 1040
  1041.1 74.1 %reduce-scatter.5.cloned.1.call-done = bf16[256,2,2,256]{0,3,2,1:T(8,128)(2,1)} async-done(((bf16[4096,2,2,256]{0,3,2,1:T(8,128)(2,1)}), bf16[256,2,2,256]{0,3,2,1:T(8,128)(2,1)}) %reduce-scatter.5.cloned.1.call-update) | async-done | bytes 524304 | tf_op jit(solution)/shard_map/reduce_scatter | solution.py:161
  (803 shorter events, 695.7 us)
Async XLA Ops:
  7.2 42.3 %all-gather.5.cloned.1.call-start = ((), (), s32[]{:S(2)}) async-start(), calls=%async_computation.3 | async-start | bytes 4456448 | tf_op jit(solution)/shard_map/all_gather | solution.py:59
  7.9 80.6 %all-gather.3.cloned.1.call-start = ((), (), s32[]{:S(2)}) async-start(), calls=%async_computation.2 | async-start | bytes 4456448 | tf_op jit(solution)/shard_map/all_gather | solution.py:58
  8.6 1030.9 %reduce-scatter.7.cloned.1.call-start = ((), (), s32[]{:S(2)}) async-start(), calls=%async_computation.5 | async-start | bytes 1114112
  116.2 14.1 %collective-permute-start = (bf16[48,4096]{1,0:T(8,128)(2,1)S(1)}, bf16[48,4096]{1,0:T(8,128)(2,1)S(1)}, u32[]{:S(2)}, u32[]{:S(2)}) collective-permute-start(bf16[48,4096]{1,0:T(8,128)(2,1)S(1)} %get-tuple-element.1734), channel_id=1, source_target_pairs={{0,16},{16,32},{32,48},{48,64},{64,80},{80,96},{96,112},{1,17},{17... | collective-permute-start | bytes 1179656 | tf_op jit(solution)/shard_map/while/body/eval_jaxpr/ppermute | solution.py:12
  135.7 13.3 %collective-permute-start = (bf16[48,4096]{1,0:T(8,128)(2,1)S(1)}, bf16[48,4096]{1,0:T(8,128)(2,1)S(1)}, u32[]{:S(2)}, u32[]{:S(2)}) collective-permute-start(bf16[48,4096]{1,0:T(8,128)(2,1)S(1)} %get-tuple-element.1734), channel_id=1, source_target_pairs={{0,16},{16,32},{32,48},{48,64},{64,80},{80,96},{96,112},{1,17},{17... | collective-permute-start | bytes 1179656 | tf_op jit(solution)/shard_map/while/body/eval_jaxpr/ppermute | solution.py:12
  154.4 12.3 %collective-permute-start = (bf16[48,4096]{1,0:T(8,128)(2,1)S(1)}, bf16[48,4096]{1,0:T(8,128)(2,1)S(1)}, u32[]{:S(2)}, u32[]{:S(2)}) collective-permute-start(bf16[48,4096]{1,0:T(8,128)(2,1)S(1)} %get-tuple-element.1734), channel_id=1, source_target_pairs={{0,16},{16,32},{32,48},{48,64},{64,80},{80,96},{96,112},{1,17},{17... | collective-permute-start | bytes 1179656 | tf_op jit(solution)/shard_map/while/body/eval_jaxpr/ppermute | solution.py:12
  167.5 16.0 %collective-permute-start = (bf16[48,4096]{1,0:T(8,128)(2,1)S(1)}, bf16[48,4096]{1,0:T(8,128)(2,1)S(1)}, u32[]{:S(2)}, u32[]{:S(2)}) collective-permute-start(bf16[48,4096]{1,0:T(8,128)(2,1)S(1)} %get-tuple-element.1734), channel_id=1, source_target_pairs={{0,16},{16,32},{32,48},{48,64},{64,80},{80,96},{96,112},{1,17},{17... | collective-permute-start | bytes 1179656 | tf_op jit(solution)/shard_map/while/body/eval_jaxpr/ppermute | solution.py:12
  196.3 16.6 %collective-permute-start = (bf16[48,4096]{1,0:T(8,128)(2,1)S(1)}, bf16[48,4096]{1,0:T(8,128)(2,1)S(1)}, u32[]{:S(2)}, u32[]{:S(2)}) collective-permute-start(bf16[48,4096]{1,0:T(8,128)(2,1)S(1)} %get-tuple-element.1734), channel_id=1, source_target_pairs={{0,16},{16,32},{32,48},{48,64},{64,80},{80,96},{96,112},{1,17},{17... | collective-permute-start | bytes 1179656 | tf_op jit(solution)/shard_map/while/body/eval_jaxpr/ppermute | solution.py:12
  252.3 12.4 %collective-permute-start = (bf16[48,4096]{1,0:T(8,128)(2,1)S(1)}, bf16[48,4096]{1,0:T(8,128)(2,1)S(1)}, u32[]{:S(2)}, u32[]{:S(2)}) collective-permute-start(bf16[48,4096]{1,0:T(8,128)(2,1)S(1)} %get-tuple-element.1734), channel_id=1, source_target_pairs={{0,16},{16,32},{32,48},{48,64},{64,80},{80,96},{96,112},{1,17},{17... | collective-permute-start | bytes 1179656 | tf_op jit(solution)/shard_map/while/body/eval_jaxpr/ppermute | solution.py:12
  266.9 18.3 %collective-permute-start.1 = (bf16[48,4096]{1,0:T(8,128)(2,1)S(1)}, bf16[48,4096]{1,0:T(8,128)(2,1)S(1)}, u32[]{:S(2)}, u32[]{:S(2)}) collective-permute-start(bf16[48,4096]{1,0:T(8,128)(2,1)S(1)} %get-tuple-element.1747), channel_id=1, source_target_pairs={{16,0},{32,16},{48,32},{64,48},{80,64},{96,80},{112,96},{17,1},{33... | collective-permute-start | bytes 1179656 | tf_op jit(solution)/shard_map/while/body/eval_jaxpr/ppermute | solution.py:12
  286.0 15.0 %collective-permute-start.1 = (bf16[48,4096]{1,0:T(8,128)(2,1)S(1)}, bf16[48,4096]{1,0:T(8,128)(2,1)S(1)}, u32[]{:S(2)}, u32[]{:S(2)}) collective-permute-start(bf16[48,4096]{1,0:T(8,128)(2,1)S(1)} %get-tuple-element.1747), channel_id=1, source_target_pairs={{16,0},{32,16},{48,32},{64,48},{80,64},{96,80},{112,96},{17,1},{33... | collective-permute-start | bytes 1179656 | tf_op jit(solution)/shard_map/while/body/eval_jaxpr/ppermute | solution.py:12
  301.9 15.6 %collective-permute-start.1 = (bf16[48,4096]{1,0:T(8,128)(2,1)S(1)}, bf16[48,4096]{1,0:T(8,128)(2,1)S(1)}, u32[]{:S(2)}, u32[]{:S(2)}) collective-permute-start(bf16[48,4096]{1,0:T(8,128)(2,1)S(1)} %get-tuple-element.1747), channel_id=1, source_target_pairs={{16,0},{32,16},{48,32},{64,48},{80,64},{96,80},{112,96},{17,1},{33... | collective-permute-start | bytes 1179656 | tf_op jit(solution)/shard_map/while/body/eval_jaxpr/ppermute | solution.py:12
  318.3 17.3 %collective-permute-start.1 = (bf16[48,4096]{1,0:T(8,128)(2,1)S(1)}, bf16[48,4096]{1,0:T(8,128)(2,1)S(1)}, u32[]{:S(2)}, u32[]{:S(2)}) collective-permute-start(bf16[48,4096]{1,0:T(8,128)(2,1)S(1)} %get-tuple-element.1747), channel_id=1, source_target_pairs={{16,0},{32,16},{48,32},{64,48},{80,64},{96,80},{112,96},{17,1},{33... | collective-permute-start | bytes 1179656 | tf_op jit(solution)/shard_map/while/body/eval_jaxpr/ppermute | solution.py:12
  336.4 16.4 %collective-permute-start.1 = (bf16[48,4096]{1,0:T(8,128)(2,1)S(1)}, bf16[48,4096]{1,0:T(8,128)(2,1)S(1)}, u32[]{:S(2)}, u32[]{:S(2)}) collective-permute-start(bf16[48,4096]{1,0:T(8,128)(2,1)S(1)} %get-tuple-element.1747), channel_id=1, source_target_pairs={{16,0},{32,16},{48,32},{64,48},{80,64},{96,80},{112,96},{17,1},{33... | collective-permute-start | bytes 1179656 | tf_op jit(solution)/shard_map/while/body/eval_jaxpr/ppermute | solution.py:12
  365.6 49.1 %collective-permute-start.1 = (bf16[48,4096]{1,0:T(8,128)(2,1)S(1)}, bf16[48,4096]{1,0:T(8,128)(2,1)S(1)}, u32[]{:S(2)}, u32[]{:S(2)}) collective-permute-start(bf16[48,4096]{1,0:T(8,128)(2,1)S(1)} %get-tuple-element.1747), channel_id=1, source_target_pairs={{16,0},{32,16},{48,32},{64,48},{80,64},{96,80},{112,96},{17,1},{33... | collective-permute-start | bytes 1179656 | tf_op jit(solution)/shard_map/while/body/eval_jaxpr/ppermute | solution.py:12
  420.7 14.0 %collective-permute-start.1 = (bf16[48,4096]{1,0:T(8,128)(2,1)S(1)}, bf16[48,4096]{1,0:T(8,128)(2,1)S(1)}, u32[]{:S(2)}, u32[]{:S(2)}) collective-permute-start(bf16[48,4096]{1,0:T(8,128)(2,1)S(1)} %get-tuple-element.1747), channel_id=1, source_target_pairs={{16,0},{32,16},{48,32},{64,48},{80,64},{96,80},{112,96},{17,1},{33... | collective-permute-start | bytes 1179656 | tf_op jit(solution)/shard_map/while/body/eval_jaxpr/ppermute | solution.py:12
  440.7 13.1 %collective-permute-start.1 = (bf16[48,4096]{1,0:T(8,128)(2,1)S(1)}, bf16[48,4096]{1,0:T(8,128)(2,1)S(1)}, u32[]{:S(2)}, u32[]{:S(2)}) collective-permute-start(bf16[48,4096]{1,0:T(8,128)(2,1)S(1)} %get-tuple-element.1747), channel_id=1, source_target_pairs={{16,0},{32,16},{48,32},{64,48},{80,64},{96,80},{112,96},{17,1},{33... | collective-permute-start | bytes 1179656 | tf_op jit(solution)/shard_map/while/body/eval_jaxpr/ppermute | solution.py:12
  523.2 12.8 %collective-permute-start.2 = (bf16[48,4096]{1,0:T(8,128)(2,1)S(1)}, bf16[48,4096]{1,0:T(8,128)(2,1)S(1)}, u32[]{:S(2)}, u32[]{:S(2)}) collective-permute-start(bf16[48,4096]{1,0:T(8,128)(2,1)S(1)} %get-tuple-element.1764), channel_id=1, source_target_pairs={{0,16},{16,32},{32,48},{48,64},{64,80},{80,96},{96,112},{1,17},{17... | collective-permute-start | bytes 1179656 | tf_op jit(solution)/shard_map/while/body/eval_jaxpr/ppermute | solution.py:12
  546.5 12.7 %collective-permute-start.2 = (bf16[48,4096]{1,0:T(8,128)(2,1)S(1)}, bf16[48,4096]{1,0:T(8,128)(2,1)S(1)}, u32[]{:S(2)}, u32[]{:S(2)}) collective-permute-start(bf16[48,4096]{1,0:T(8,128)(2,1)S(1)} %get-tuple-element.1764), channel_id=1, source_target_pairs={{0,16},{16,32},{32,48},{48,64},{64,80},{80,96},{96,112},{1,17},{17... | collective-permute-start | bytes 1179656 | tf_op jit(solution)/shard_map/while/body/eval_jaxpr/ppermute | solution.py:12
  582.5 19.8 %collective-permute-start.2 = (bf16[48,4096]{1,0:T(8,128)(2,1)S(1)}, bf16[48,4096]{1,0:T(8,128)(2,1)S(1)}, u32[]{:S(2)}, u32[]{:S(2)}) collective-permute-start(bf16[48,4096]{1,0:T(8,128)(2,1)S(1)} %get-tuple-element.1764), channel_id=1, source_target_pairs={{0,16},{16,32},{32,48},{48,64},{64,80},{80,96},{96,112},{1,17},{17... | collective-permute-start | bytes 1179656 | tf_op jit(solution)/shard_map/while/body/eval_jaxpr/ppermute | solution.py:12
  616.0 26.7 %collective-permute-start.2 = (bf16[48,4096]{1,0:T(8,128)(2,1)S(1)}, bf16[48,4096]{1,0:T(8,128)(2,1)S(1)}, u32[]{:S(2)}, u32[]{:S(2)}) collective-permute-start(bf16[48,4096]{1,0:T(8,128)(2,1)S(1)} %get-tuple-element.1764), channel_id=1, source_target_pairs={{0,16},{16,32},{32,48},{48,64},{64,80},{80,96},{96,112},{1,17},{17... | collective-permute-start | bytes 1179656 | tf_op jit(solution)/shard_map/while/body/eval_jaxpr/ppermute | solution.py:12
  643.6 15.7 %collective-permute-start.2 = (bf16[48,4096]{1,0:T(8,128)(2,1)S(1)}, bf16[48,4096]{1,0:T(8,128)(2,1)S(1)}, u32[]{:S(2)}, u32[]{:S(2)}) collective-permute-start(bf16[48,4096]{1,0:T(8,128)(2,1)S(1)} %get-tuple-element.1764), channel_id=1, source_target_pairs={{0,16},{16,32},{32,48},{48,64},{64,80},{80,96},{96,112},{1,17},{17... | collective-permute-start | bytes 1179656 | tf_op jit(solution)/shard_map/while/body/eval_jaxpr/ppermute | solution.py:12
  660.2 16.3 %collective-permute-start.2 = (bf16[48,4096]{1,0:T(8,128)(2,1)S(1)}, bf16[48,4096]{1,0:T(8,128)(2,1)S(1)}, u32[]{:S(2)}, u32[]{:S(2)}) collective-permute-start(bf16[48,4096]{1,0:T(8,128)(2,1)S(1)} %get-tuple-element.1764), channel_id=1, source_target_pairs={{0,16},{16,32},{32,48},{48,64},{64,80},{80,96},{96,112},{1,17},{17... | collective-permute-start | bytes 1179656 | tf_op jit(solution)/shard_map/while/body/eval_jaxpr/ppermute | solution.py:12
  677.4 12.3 %collective-permute-start.2 = (bf16[48,4096]{1,0:T(8,128)(2,1)S(1)}, bf16[48,4096]{1,0:T(8,128)(2,1)S(1)}, u32[]{:S(2)}, u32[]{:S(2)}) collective-permute-start(bf16[48,4096]{1,0:T(8,128)(2,1)S(1)} %get-tuple-element.1764), channel_id=1, source_target_pairs={{0,16},{16,32},{32,48},{48,64},{64,80},{80,96},{96,112},{1,17},{17... | collective-permute-start | bytes 1179656 | tf_op jit(solution)/shard_map/while/body/eval_jaxpr/ppermute | solution.py:12
  690.6 14.4 %collective-permute-start.2 = (bf16[48,4096]{1,0:T(8,128)(2,1)S(1)}, bf16[48,4096]{1,0:T(8,128)(2,1)S(1)}, u32[]{:S(2)}, u32[]{:S(2)}) collective-permute-start(bf16[48,4096]{1,0:T(8,128)(2,1)S(1)} %get-tuple-element.1764), channel_id=1, source_target_pairs={{0,16},{16,32},{32,48},{48,64},{64,80},{80,96},{96,112},{1,17},{17... | collective-permute-start | bytes 1179656 | tf_op jit(solution)/shard_map/while/body/eval_jaxpr/ppermute | solution.py:12
  709.8 14.3 %collective-permute-start.3 = (bf16[48,4096]{1,0:T(8,128)(2,1)S(1)}, bf16[48,4096]{1,0:T(8,128)(2,1)S(1)}, u32[]{:S(2)}, u32[]{:S(2)}) collective-permute-start(bf16[48,4096]{1,0:T(8,128)(2,1)S(1)} %get-tuple-element.1788), channel_id=1, source_target_pairs={{16,0},{32,16},{48,32},{64,48},{80,64},{96,80},{112,96},{17,1},{33... | collective-permute-start | bytes 1179656 | tf_op jit(solution)/shard_map/while/body/eval_jaxpr/ppermute | solution.py:12
  725.0 15.1 %collective-permute-start.3 = (bf16[48,4096]{1,0:T(8,128)(2,1)S(1)}, bf16[48,4096]{1,0:T(8,128)(2,1)S(1)}, u32[]{:S(2)}, u32[]{:S(2)}) collective-permute-start(bf16[48,4096]{1,0:T(8,128)(2,1)S(1)} %get-tuple-element.1788), channel_id=1, source_target_pairs={{16,0},{32,16},{48,32},{64,48},{80,64},{96,80},{112,96},{17,1},{33... | collective-permute-start | bytes 1179656 | tf_op jit(solution)/shard_map/while/body/eval_jaxpr/ppermute | solution.py:12
  753.7 15.1 %collective-permute-start.3 = (bf16[48,4096]{1,0:T(8,128)(2,1)S(1)}, bf16[48,4096]{1,0:T(8,128)(2,1)S(1)}, u32[]{:S(2)}, u32[]{:S(2)}) collective-permute-start(bf16[48,4096]{1,0:T(8,128)(2,1)S(1)} %get-tuple-element.1788), channel_id=1, source_target_pairs={{16,0},{32,16},{48,32},{64,48},{80,64},{96,80},{112,96},{17,1},{33... | collective-permute-start | bytes 1179656 | tf_op jit(solution)/shard_map/while/body/eval_jaxpr/ppermute | solution.py:12
  782.6 22.2 %collective-permute-start.3 = (bf16[48,4096]{1,0:T(8,128)(2,1)S(1)}, bf16[48,4096]{1,0:T(8,128)(2,1)S(1)}, u32[]{:S(2)}, u32[]{:S(2)}) collective-permute-start(bf16[48,4096]{1,0:T(8,128)(2,1)S(1)} %get-tuple-element.1788), channel_id=1, source_target_pairs={{16,0},{32,16},{48,32},{64,48},{80,64},{96,80},{112,96},{17,1},{33... | collective-permute-start | bytes 1179656 | tf_op jit(solution)/shard_map/while/body/eval_jaxpr/ppermute | solution.py:12
  805.8 85.6 %collective-permute-start.3 = (bf16[48,4096]{1,0:T(8,128)(2,1)S(1)}, bf16[48,4096]{1,0:T(8,128)(2,1)S(1)}, u32[]{:S(2)}, u32[]{:S(2)}) collective-permute-start(bf16[48,4096]{1,0:T(8,128)(2,1)S(1)} %get-tuple-element.1788), channel_id=1, source_target_pairs={{16,0},{32,16},{48,32},{64,48},{80,64},{96,80},{112,96},{17,1},{33... | collective-permute-start | bytes 1179656 | tf_op jit(solution)/shard_map/while/body/eval_jaxpr/ppermute | solution.py:12
  944.6 13.2 %collective-permute-start.3 = (bf16[48,4096]{1,0:T(8,128)(2,1)S(1)}, bf16[48,4096]{1,0:T(8,128)(2,1)S(1)}, u32[]{:S(2)}, u32[]{:S(2)}) collective-permute-start(bf16[48,4096]{1,0:T(8,128)(2,1)S(1)} %get-tuple-element.1788), channel_id=1, source_target_pairs={{16,0},{32,16},{48,32},{64,48},{80,64},{96,80},{112,96},{17,1},{33... | collective-permute-start | bytes 1179656 | tf_op jit(solution)/shard_map/while/body/eval_jaxpr/ppermute | solution.py:12
  982.0 133.3 %reduce-scatter.5.cloned.1.call-start = ((), (), s32[]{:S(2)}) async-start(), calls=%async_computation.4 | async-start | bytes 8912896 | tf_op jit(solution)/shard_map/reduce_scatter | solution.py:161
  (113 other events, 376.2 us)
Sparse Core Ops, SparseCore 0:
  9.7 39.7 all-gather.4
  51.1 37.3 all-gather.2
  982.1 57.4 reduce-scatter.6
  1042.0 73.2 reduce-scatter.4
where the time goes:
time: 1130 us; the launch traced here: 1120 us
  waiting for transfers between devices  511 us (45%)
  starting transfers between devices  189 us (17%)
  local copies, waits for them, and re-layouts  169 us (15%)
  other arithmetic  150 us (13%)
  matrix products  69.6 us (6%)
  blocking collectives  20 us (2%)
  between operations  13.9 us (1%)
    ppermute x44, waiting for transfers between devices, from_behind(): lax.ppermute(value, axis, [(source, source + steps) for source in range(f...  335 us
    ppermute x44, starting transfers between devices, from_behind(): lax.ppermute(value, axis, [(source, source + steps) for source in range(f...  188 us
    dynamic_slice x132, local copies, waits for them, and re-layouts, fetch_row(): return lax.dynamic_index_in_dim(buffer, slot_index, 0, keepdims=False)  107 us
    dynamic_update_slice x77, other arithmetic, advance(): lax.dynamic_update_index_in_dim(buffer, jnp.where(in_range, fresh_row, fe...  78.8 us
    reduce_scatter x1, waiting for transfers between devices, per_device(): lax.psum_scatter(jnp.stack([in_block, out_block], 1).astype(jnp.bfloat16)...  74.1 us
    unnamed x5, waiting for transfers between devices  46.4 us
    all_gather x1, waiting for transfers between devices, per_device(): lax.all_gather(w_in, 'dp', axis=2, tiled=True)  34.6 us
    dot_general x8, matrix products, layer_forward(): lax.dot_general(lifted, w_out, (((1,), (1,)), ((), ())), preferred_elemen...  29.4 us
  transfers between devices with their start and end apart: 48, of which 42 were waited for; matrix products, arithmetic and copies ran while one was open for 18% of the time, Pallas kernels for 0%

commit v1 on v0

v1 whole, which is shorter than its diff:
```python
import functools

import jax
import jax.numpy as jnp
from jax import lax
from jax.experimental import pallas as pl
from jax.experimental.pallas import tpu as pltpu
from jax.sharding import Mesh, PartitionSpec as P

EPS = 1e-06
PARTS = 2
STAGES = 4
DEPTH = 4
PLANE = ("yh", "yl", "x", "c")
SPLIT = 2
bf16, f32 = jnp.bfloat16, jnp.float32


def narrow_t(left, right):
    return lax.dot_general(left, right, (((1,), (1,)), ((), ())), preferred_element_type=f32)


def square_mean_inverse(rows):
    return lax.rsqrt(jnp.mean(rows * rows, axis=-1, keepdims=True) + EPS)


def forward_kernel(info, feed, incoming, weights, _, __, outgoing, kept_x, kept_act, xs, acc, inv, lifted):
    step = pl.program_id(0)
    active = info[0] == 1
    part = lax.rem(step, 4)
    half = xs.shape[1] // SPLIT
    block = weights[...].reshape(half, weights.shape[-1])

    @pl.when(jnp.logical_and(active, step == 0))
    def _load():
        first = info[3] == 1

        @pl.when(first)
        def _feed():
            xs[...] = feed[0].astype(f32)

        @pl.when(jnp.logical_not(first))
        def _received():
            xs[...] = incoming[...].astype(f32)

    @pl.when(jnp.logical_and(active, part == 0))
    def _in0():
        rows = xs[...].astype(bf16)
        kept_x[0, 0] = rows
        inv[...] = jnp.broadcast_to(square_mean_inverse(rows.astype(f32)), inv.shape)
        acc[...] = jnp.dot(rows[:, :half], block, preferred_element_type=f32)

    @pl.when(jnp.logical_and(active, part == 1))
    def _in1():
        total = acc[...] + jnp.dot(kept_x[0, 0, :, half:], block, preferred_element_type=f32)
        act = total * inv[:, :1]
        kept_act[0, 0] = act
        lifted[...] = (act * jax.nn.sigmoid(act)).astype(bf16)

    @pl.when(jnp.logical_and(active, part == 2))
    def _out0():
        xs[:, :half] = xs[:, :half] + narrow_t(lifted[...], block)

    @pl.when(jnp.logical_and(active, part == 3))
    def _out1():
        xs[:, half:] = xs[:, half:] + narrow_t(lifted[...], block)

    @pl.when(jnp.logical_and(active, step == 4 * DEPTH - 1))
    def _store():
        outgoing[...] = xs[...].astype(bf16)


def backward_kernel(
    info, feed, incoming, weights, kept_x, kept_act, _, __, ___,
    outgoing, kept_u, kept_h, kept_l, us, acc, coef, narrow,
):
    step = pl.program_id(0)
    active = info[0] == 1
    part = lax.rem(step, 4)
    half = us.shape[1] // SPLIT
    block = weights[...].reshape(half, weights.shape[-1])

    @pl.when(jnp.logical_and(active, step == 0))
    def _load():
        first = info[3] == 1

        @pl.when(first)
        def _feed():
            us[...] = feed[0].astype(f32)

        @pl.when(jnp.logical_not(first))
        def _received():
            us[...] = incoming[...].astype(f32)

    @pl.when(jnp.logical_and(active, part == 0))
    def _out0():
        rows = us[...].astype(bf16)
        kept_u[0, 0] = rows
        acc[...] = jnp.dot(rows[:, :half], block, preferred_element_type=f32)

    @pl.when(jnp.logical_and(active, part == 1))
    def _out1():
        grad_lift = acc[...] + jnp.dot(kept_u[0, 0, :, half:], block, preferred_element_type=f32)
        act = kept_act[0, 0]
        inv = square_mean_inverse(kept_x[0, 0].astype(f32))
        logistic = jax.nn.sigmoid(act)
        grad_act = grad_lift * logistic * (1.0 + act * (1.0 - logistic))
        scaled = (grad_act * inv).astype(bf16)
        narrow[...] = scaled
        kept_h[0, 0] = scaled
        kept_l[0, 0] = (act * logistic).astype(bf16)
        weight = jnp.sum(grad_act * act, axis=-1, keepdims=True) * (inv * inv) * (1.0 / us.shape[1])
        coef[...] = jnp.broadcast_to(weight, coef.shape)

    @pl.when(jnp.logical_and(active, part == 2))
    def _in0():
        us[:, :half] = us[:, :half] + narrow_t(narrow[...], block) - kept_x[0, 0, :, :half].astype(f32) * coef[:, :1]

    @pl.when(jnp.logical_and(active, part == 3))
    def _in1():
        us[:, half:] = us[:, half:] + narrow_t(narrow[...], block) - kept_x[0, 0, :, half:].astype(f32) * coef[:, :1]

    @pl.when(jnp.logical_and(active, step == 4 * DEPTH - 1))
    def _store():
        outgoing[...] = us[...].astype(bf16)


def grads_kernel(info, kept_x, kept_u, kept_h, kept_l, out):
    which = pl.program_id(1)
    rows = kept_x.shape[0] * kept_x.shape[2]

    def product(wide, thin):
        left = wide[...].reshape(rows, wide.shape[-1])
        right = thin[...].reshape(rows, thin.shape[-1])
        made = lax.dot_general(left, right, (((0,), (0,)), ((), ())), preferred_element_type=f32)
        out[...] = made.astype(bf16).reshape(out.shape)

    @pl.when(which == 0)
    def _in():
        product(kept_x, kept_h)

    @pl.when(which == 1)
    def _out():
        product(kept_u, kept_l)


def layer_of(info, place):
    return jnp.where(info[2] == 0, place, DEPTH - 1 - place)


def weight_spec(block_count, per_block, lowrank, forward):
    def index(step, info):
        place = step // 4
        side = lax.rem(step, 4) // 2
        if not forward:
            place, side = DEPTH - 1 - place, 1 - side
        layer = layer_of(info, place)
        spot = (lax.rem(layer, 2), lax.rem(step, SPLIT), layer // 2, side, 0, 0)
        return tuple(jnp.where(info[0] == 1, s, 0) for s in spot)

    return pl.BlockSpec((1, block_count // SPLIT, 1, 1, per_block, lowrank), index)


def place_of(step, forward):
    return step // 4 if forward else DEPTH - 1 - step // 4


def kept_spec(rows, width, forward):
    return pl.BlockSpec((1, 1, rows, width), lambda step, info: (info[1], place_of(step, forward), 0, 0))


def feed_spec(rows, width, parts):
    return pl.BlockSpec((1, rows, width), lambda step, info: (jnp.minimum(info[1], parts - 1), 0, 0))


def whole_spec(rows, width):
    return pl.BlockSpec((rows, width), lambda step, info: (0, 0))


ANY = pl.BlockSpec(memory_space=pl.ANY)


def shape_of(array):
    return jax.ShapeDtypeStruct(array.shape, array.dtype)


def forward_visit(info, feed, incoming, weights, kept_x, kept_act):
    parts, rows, width = feed.shape
    lowrank = weights.shape[-1]
    return pl.pallas_call(
        forward_kernel,
        grid_spec=pltpu.PrefetchScalarGridSpec(
            num_scalar_prefetch=1,
            grid=(4 * DEPTH,),
            in_specs=[
                feed_spec(rows, width, parts),
                whole_spec(rows, width),
                weight_spec(weights.shape[1], weights.shape[-2], lowrank, True),
                ANY,
                ANY,
            ],
            out_specs=[
                whole_spec(rows, width),
                kept_spec(rows, width, True),
                kept_spec(rows, lowrank, True),
            ],
            scratch_shapes=[
                pltpu.VMEM((rows, width), f32),
                pltpu.VMEM((rows, lowrank), f32),
                pltpu.VMEM((rows, 128), f32),
                pltpu.VMEM((rows, lowrank), bf16),
            ],
        ),
        out_shape=[jax.ShapeDtypeStruct((rows, width), bf16), shape_of(kept_x), shape_of(kept_act)],
        input_output_aliases={4: 1, 5: 2},
        compiler_params=pltpu.CompilerParams(vmem_limit_bytes=24 * 1024 * 1024),
        cost_estimate=pl.CostEstimate(flops=2 * DEPTH * 2 * rows * width * lowrank, bytes_accessed=weights.size * 2, transcendentals=0),
        name="forward_visit",
    )(info, feed, incoming, weights, kept_x, kept_act)


def backward_visit(info, feed, incoming, weights, kept_x, kept_act, kept_u, kept_h, kept_l):
    parts, rows, width = feed.shape
    lowrank = weights.shape[-1]
    return pl.pallas_call(
        backward_kernel,
        grid_spec=pltpu.PrefetchScalarGridSpec(
            num_scalar_prefetch=1,
            grid=(4 * DEPTH,),
            in_specs=[
                feed_spec(rows, width, parts),
                whole_spec(rows, width),
                weight_spec(weights.shape[1], weights.shape[-2], lowrank, False),
                kept_spec(rows, width, False),
                kept_spec(rows, lowrank, False),
                ANY,
                ANY,
                ANY,
            ],
            out_specs=[
                whole_spec(rows, width),
                kept_spec(rows, width, False),
                kept_spec(rows, lowrank, False),
                kept_spec(rows, lowrank, False),
            ],
            scratch_shapes=[
                pltpu.VMEM((rows, width), f32),
                pltpu.VMEM((rows, lowrank), f32),
                pltpu.VMEM((rows, 128), f32),
                pltpu.VMEM((rows, lowrank), bf16),
            ],
        ),
        out_shape=[
            jax.ShapeDtypeStruct((rows, width), bf16),
            shape_of(kept_u),
            shape_of(kept_h),
            shape_of(kept_l),
        ],
        input_output_aliases={6: 1, 7: 2, 8: 3},
        compiler_params=pltpu.CompilerParams(vmem_limit_bytes=24 * 1024 * 1024),
        cost_estimate=pl.CostEstimate(flops=2 * DEPTH * 2 * rows * width * lowrank, bytes_accessed=weights.size * 2, transcendentals=0),
        name="backward_visit",
    )(info, feed, incoming, weights, kept_x, kept_act, kept_u, kept_h, kept_l)


def weight_grads(info, kept_x, kept_u, kept_h, kept_l, parts, weights):
    rows, width = kept_x.shape[2:]
    lowrank = kept_h.shape[-1]
    wide = pl.BlockSpec((parts, 1, rows, width // SPLIT), lambda q, io, ch, info: (0, layer_of(info, q), 0, ch))
    thin = pl.BlockSpec((parts, 1, rows, lowrank), lambda q, io, ch, info: (0, layer_of(info, q), 0, 0))
    return pl.pallas_call(
        grads_kernel,
        grid_spec=pltpu.PrefetchScalarGridSpec(
            num_scalar_prefetch=1,
            grid=(DEPTH, 2, SPLIT),
            in_specs=[wide, wide, thin, thin],
            out_specs=pl.BlockSpec(
                (1, weights.shape[1] // SPLIT, 1, 1) + weights.shape[-2:],
                lambda q, io, ch, info: (lax.rem(q, 2), ch, q // 2, io, 0, 0),
            ),
        ),
        out_shape=shape_of(weights),
        compiler_params=pltpu.CompilerParams(vmem_limit_bytes=32 * 1024 * 1024),
        name="weight_grads",
    )(info, kept_x, kept_u, kept_h, kept_l)


def per_device(inputs, cotangent, w_in, w_out, norm_gain):
    batches, tok_rows, features = inputs.shape
    own_rows, lowrank = w_in.shape[2:]
    z, yh = lax.axis_index("z"), lax.axis_index("yh")
    low = lax.rem(z, 2)
    leg = jnp.where(jnp.logical_or(z == 0, z == STAGES - 1), 0, 1)
    stage = lax.rem(STAGES - z, STAGES)
    pairs = [(i, i ^ 1) for i in range(STAGES)]

    gain = norm_gain[:, 0].astype(f32)[:, :, None]
    wide_in = w_in[:, 0].astype(f32)
    both = jnp.stack([(wide_in * gain).astype(bf16), w_out[:, 0]], 1)
    keep = lax.dynamic_index_in_dim(both, leg, 0, keepdims=False)
    other = lax.ppermute(lax.dynamic_index_in_dim(both, 1 - leg, 0, keepdims=False), "z", pairs)
    local = jnp.where(low == 0, jnp.stack([keep, other]), jnp.stack([other, keep]))
    weights = lax.all_gather(local, PLANE, axis=0, tiled=False)
    blocks = weights.shape[0] // 2
    weights = weights.reshape((2, blocks) + weights.shape[1:])

    share = batches // 2 * tok_rows
    rows = share // PARTS

    def mine(array):
        piece = lax.dynamic_slice_in_dim(array, yh * (batches // 2), batches // 2, 0)
        return piece.reshape(PARTS, rows, features)

    feed, cot = mine(inputs), mine(cotangent)
    kept_x = jnp.zeros((PARTS + 1, DEPTH, rows, features), bf16)
    kept_act = jnp.zeros((PARTS + 1, DEPTH, rows, lowrank), f32)
    kept_u = jnp.zeros((PARTS + 1, DEPTH, rows, features), bf16)
    kept_h = jnp.zeros((PARTS + 1, DEPTH, rows, lowrank), bf16)
    kept_l = jnp.zeros((PARTS + 1, DEPTH, rows, lowrank), bf16)

    def info_for(part, first):
        active = jnp.logical_and(part >= 0, part < PARTS)
        return jnp.stack(
            [active.astype(jnp.int32), jnp.where(active, part, PARTS), leg, first.astype(jnp.int32)]
        ).astype(jnp.int32)

    onward = [(z_from, (z_from - 1) % STAGES) for z_from in (0, 3, 2)]
    homeward = [(b, a) for a, b in onward]
    coming, returning = feed[0], cot[0]
    for tick in range(PARTS + 2 * STAGES - 2):
        do_forward = tick < PARTS + STAGES - 1
        do_backward = tick >= STAGES - 1
        if do_forward:
            info = info_for(tick - stage, stage == 0)
            if tick > STAGES - 1:
                info, kept_h = lax.optimization_barrier((info, kept_h))
            coming, kept_x, kept_act = forward_visit(info, feed, coming, weights, kept_x, kept_act)
            if tick < PARTS + STAGES - 2:
                coming = lax.ppermute(coming, "z", onward)
        if do_backward:
            info = info_for(tick - (2 * STAGES - 2) + stage, stage == STAGES - 1)
            returning, kept_u, kept_h, kept_l = backward_visit(
                info, cot, returning, weights, kept_x, kept_act, kept_u, kept_h, kept_l
            )
            if tick < PARTS + 2 * STAGES - 3:
                returning = lax.ppermute(returning, "z", homeward)

    grads = weight_grads(info, kept_x, kept_u, kept_h, kept_l, PARTS, weights)
    grads = grads.reshape((2 * blocks,) + grads.shape[2:])
    owned = lax.psum_scatter(grads, PLANE, scatter_dimension=0, tiled=True)[0]
    kept = lax.dynamic_index_in_dim(owned, low, 0, keepdims=False)
    swapped = lax.ppermute(lax.dynamic_index_in_dim(owned, 1 - low, 0, keepdims=False), "z", pairs)
    legs = jnp.where(leg == 0, jnp.stack([kept, swapped]), jnp.stack([swapped, kept])).astype(f32)
    grad_in = legs[:, 0] * gain
    gain_grad = jnp.sum(legs[:, 0] * wide_in, axis=-1)
    return grad_in[:, None], legs[:, 1][:, None], gain_grad[:, None]


def solution(mesh):
    fine = Mesh(mesh.devices.reshape(STAGES, 2, 2, 4, 2), ("z",) + PLANE)
    sec, dp = ("z", "yh"), ("yl", "x", "c")
    return jax.shard_map(
        per_device,
        mesh=fine,
        in_specs=(
            P(None, dp, None),
            P(None, dp, None),
            P(None, sec, dp, None),
            P(None, sec, dp, None),
            P(None, sec, dp),
        ),
        out_specs=(
            P(None, sec, dp, None),
            P(None, sec, dp, None),
            P(None, sec, dp),
        ),
        check_vma=False,
    )
```

time: 1130 us -> 501 us (0.44)
  waiting for transfers between devices: 511 us -> 279 us
  starting transfers between devices: 189 us -> 35 us
  other arithmetic: 150 us -> 5.7 us
  local copies, waits for them, and re-layouts: 169 us -> 81.1 us
  Pallas kernels: 0 us -> 84.2 us
  matrix products: 69.6 us -> 0 us
  blocking collectives: 20 us -> 0 us
    ppermute x44 -> x10, waiting for transfers between devices: 335 us -> 92.7 us  [the longest x4 56.9 us: per_device(): returning = lax.ppermute(returning, 'z', homeward)]
    ppermute x44 -> x10, starting transfers between devices: 188 us -> 34.9 us  [the longest x4 25.9 us: per_device(): coming = lax.ppermute(coming, 'z', onward)]
    dynamic_slice x132 -> x3, local copies, waits for them, and re-layouts: 107 us -> 1.19 us  [the longest x1 1.06 us: per_device(): kept = lax.dynamic_index_in_dim(owned, low, 0, keepdims=False)]
    pallas_call x0 -> x11, Pallas kernels: none -> 84.2 us  [the longest x5 38 us: backward_visit(): pl.pallas_call(backward_kernel, grid_spec=pltpu.PrefetchScalarGridSpec(nu...]
    dynamic_update_slice x77 -> x0, other arithmetic: 78.8 us -> none  [advance(): lax.dynamic_update_index_in_dim(buffer, jnp.where(in_range, fresh_row, fe...]
    unnamed x15 -> x60, local copies, waits for them, and re-layouts: 4.95 us -> 78.1 us
    dot_general x34 -> x0, matrix products: 69.6 us -> none  [the longest x8 29.4 us: layer_forward(): lax.dot_general(lifted, w_out, (((1,), (1,)), ((), ())), preferred_elemen...]
    unnamed x5 -> x2, waiting for transfers between devices: 46.4 us -> 0.03 us
  transfers between devices with their start and end apart: 48 -> 12, of which waited for: 42 -> 10; matrix products, arithmetic and copies ran while one was open for 18% -> 0% of each run, Pallas kernels for 0% -> 2%
where the time goes in v1:
time: 501 us; the launch traced here: 500 us
  waiting for transfers between devices  279 us (56%)
  Pallas kernels  84.2 us (17%)
  local copies, waits for them, and re-layouts  81.1 us (16%)
  starting transfers between devices  35 us (7%)
  between operations  14.4 us (3%)
  other arithmetic  5.7 us (1%)
    reduce_scatter x1, waiting for transfers between devices, per_device(): owned = lax.psum_scatter(grads, PLANE, scatter_dimension=0, tiled=True)[0]  112 us
    unnamed x60, local copies, waits for them, and re-layouts  78.1 us
    all_gather x1, waiting for transfers between devices, per_device(): weights = lax.all_gather(local, PLANE, axis=0, tiled=False)  74.4 us
    ppermute x4, waiting for transfers between devices, per_device(): returning = lax.ppermute(returning, 'z', homeward)  56.9 us
    pallas_call x5, Pallas kernels, backward_visit(): pl.pallas_call(backward_kernel, grid_spec=pltpu.PrefetchScalarGridSpec(nu...  38 us
    pallas_call x5, Pallas kernels, forward_visit(): pl.pallas_call(forward_kernel, grid_spec=pltpu.PrefetchScalarGridSpec(num...  32.4 us
    ppermute x4, starting transfers between devices, per_device(): coming = lax.ppermute(coming, 'z', onward)  25.9 us
    ppermute x4, waiting for transfers between devices, per_device(): coming = lax.ppermute(coming, 'z', onward)  24.2 us
  transfers between devices with their start and end apart: 12, of which 10 were waited for; matrix products, arithmetic and copies ran while one was open for 0% of the time, Pallas kernels for 2%

profile of v1, /device:TPU:0, one launch (start us, length us, event | category | flops | bytes accessed | tf_op | source)
XLA Modules:
  0.0 499.8 jit_solution(18335089440123862391)
XLA Ops:
  12.2 6.3 %collective-permute-done = bf16[2,256,256]{2,1,0:T(8,128)(2,1)S(1)} collective-permute-done((bf16[2,256,256]{2,1,0:T(8,128)(2,1)S(1)}, bf16[2,256,256]{2,1,0:T(8,128)(2,1)S(1)}, u32[]{:S(2)}, u32[]{:S(2)}) %collective-permute-start) | collective-permute-done | bytes 262176 | tf_op jit(solution)/shard_map/ppermute | solution.py:301
  19.7 74.4 %all-gather.2.cloned.1.call-done = bf16[32,2,2,256,256]{4,3,2,1,0:T(8,128)(2,1)} async-done(((bf16[1,2,2,256,256]{4,3,2,1,0:T(8,128)(2,1)}), bf16[32,2,2,256,256]{4,3,2,1,0:T(8,128)(2,1)}) %all-gather.2.cloned.1.call-update) | async-done | bytes 16777232 | tf_op jit(solution)/shard_map/all_gather | solution.py:303
  94.8 5.8 %copy-done.1 = bf16[32,2,2,256,256]{4,3,2,1,0:T(8,128)(2,1)S(1)} copy-done((bf16[32,2,2,256,256]{4,3,2,1,0:T(8,128)(2,1)S(1)}, bf16[32,2,2,256,256]{4,3,2,1,0:T(8,128)(2,1)}, u32[]{:S(2)}) %copy-start.1) | copy-done | bytes 16777240
  100.5 10.1 %forward_visit.5 = (bf16[48,4096]{1,0:T(8,128)(2,1)S(1)}, bf16[3,4,48,4096]{3,2,1,0:T(8,128)(2,1)S(1)}, f32[3,4,48,256]{3,2,1,0:T(8,128)S(1)}) custom-call(s32[4]{0:T(128)S(1)} %get-tuple-element.81.info, bf16[2,48,4096]{2,1,0:T(8,128)(2,1)S(1)} %constant_dynamic-slice_fusion.feed, ...), custom_call_target="tpu_custom_call", output_to_operand_aliasing={{1}: (4, {}), {2}: (5, {})} | custom-call | flops 805306368 | bytes 16777216 | tf_op jit(solution)/shard_map/forward_visit/pallas_call | solution.py:190
  112.3 8.7 %collective-permute-done.1.incoming = bf16[48,4096]{1,0:T(8,128)(2,1)S(1)} collective-permute-done((bf16[48,4096]{1,0:T(8,128)(2,1)S(1)}, bf16[48,4096]{1,0:T(8,128)(2,1)S(1)}, u32[]{:S(2)}, u32[]{:S(2)}) %collective-permute-start.1) | collective-permute-done | bytes 393248 | tf_op jit(solution)/shard_map/ppermute | solution.py:339
  121.0 5.8 %copy-done.2 = bf16[32,2,2,256,256]{4,3,2,1,0:T(8,128)(2,1)S(1)} copy-done((bf16[32,2,2,256,256]{4,3,2,1,0:T(8,128)(2,1)S(1)}, bf16[32,2,2,256,256]{4,3,2,1,0:T(8,128)(2,1)}, u32[]{:S(2)}) %copy-start.2) | copy-done | bytes 16777240
  126.8 10.1 %forward_visit.6 = (bf16[48,4096]{1,0:T(8,128)(2,1)S(1)}, bf16[3,4,48,4096]{3,2,1,0:T(8,128)(2,1)S(1)}, f32[3,4,48,256]{3,2,1,0:T(8,128)S(1)}) custom-call(s32[4]{0:T(128)S(1)} %add_add_fusion.5.info, bf16[2,48,4096]{2,1,0:T(8,128)(2,1)S(1)} %constant_dynamic-slice_fusion.feed, ...), custom_call_target="tpu_custom_call", output_to_operand_aliasing={{1}: (4, {}), {2}: (5, {})} | custom-call | flops 805306368 | bytes 16777216 | tf_op jit(solution)/shard_map/forward_visit/pallas_call | solution.py:190
  136.9 5.6 %collective-permute-start.2 = (bf16[48,4096]{1,0:T(8,128)(2,1)S(1)}, bf16[48,4096]{1,0:T(8,128)(2,1)S(1)}, u32[]{:S(2)}, u32[]{:S(2)}) collective-permute-start(bf16[48,4096]{1,0:T(8,128)(2,1)S(1)} %get-tuple-element.41), channel_id=1, source_target_pairs={{0,96},{96,64},{64,32},{1,97},{97,65},{65,33},{2,98},{98,66},{66,3... | collective-permute-start | bytes 1179656 | tf_op jit(solution)/shard_map/ppermute | solution.py:339
  142.6 8.2 %collective-permute-done.2.incoming = bf16[48,4096]{1,0:T(8,128)(2,1)S(1)} collective-permute-done((bf16[48,4096]{1,0:T(8,128)(2,1)S(1)}, bf16[48,4096]{1,0:T(8,128)(2,1)S(1)}, u32[]{:S(2)}, u32[]{:S(2)}) %collective-permute-start.2) | collective-permute-done | bytes 393248 | tf_op jit(solution)/shard_map/ppermute | solution.py:339
  150.8 3.1 forward_visit.7
  154.0 12.6 %collective-permute-start.3 = (bf16[48,4096]{1,0:T(8,128)(2,1)S(1)}, bf16[48,4096]{1,0:T(8,128)(2,1)S(1)}, u32[]{:S(2)}, u32[]{:S(2)}) collective-permute-start(bf16[48,4096]{1,0:T(8,128)(2,1)S(1)} %get-tuple-element.44), channel_id=1, source_target_pairs={{0,96},{96,64},{64,32},{1,97},{97,65},{65,33},{2,98},{98,66},{66,3... | collective-permute-start | bytes 1179656 | tf_op jit(solution)/shard_map/ppermute | solution.py:339
  166.6 7.3 %collective-permute-done.3.incoming = bf16[48,4096]{1,0:T(8,128)(2,1)S(1)} collective-permute-done((bf16[48,4096]{1,0:T(8,128)(2,1)S(1)}, bf16[48,4096]{1,0:T(8,128)(2,1)S(1)}, u32[]{:S(2)}, u32[]{:S(2)}) %collective-permute-start.3) | collective-permute-done | bytes 393248 | tf_op jit(solution)/shard_map/ppermute | solution.py:339
  173.9 3.9 forward_visit.8
  177.8 6.3 %collective-permute-start.4 = (bf16[48,4096]{1,0:T(8,128)(2,1)}, bf16[48,4096]{1,0:T(8,128)(2,1)}, u32[]{:S(2)}, u32[]{:S(2)}) collective-permute-start(bf16[48,4096]{1,0:T(8,128)(2,1)} %get-tuple-element.51), channel_id=1, source_target_pairs={{0,96},{96,64},{64,32},{1,97},{97,65},{65,33},{2,98},{98,66},{66,3... | collective-permute-start | bytes 1179656 | tf_op jit(solution)/shard_map/ppermute | solution.py:339
  184.8 5.8 %copy-done.3 = bf16[32,2,2,256,256]{4,3,2,1,0:T(8,128)(2,1)S(1)} copy-done((bf16[32,2,2,256,256]{4,3,2,1,0:T(8,128)(2,1)S(1)}, bf16[32,2,2,256,256]{4,3,2,1,0:T(8,128)(2,1)}, u32[]{:S(2)}) %copy-start.3) | copy-done | bytes 16777240
  190.6 3.9 backward_visit.5
  198.0 5.8 %copy-done.4 = bf16[32,2,2,256,256]{4,3,2,1,0:T(8,128)(2,1)S(1)} copy-done((bf16[32,2,2,256,256]{4,3,2,1,0:T(8,128)(2,1)S(1)}, bf16[32,2,2,256,256]{4,3,2,1,0:T(8,128)(2,1)}, u32[]{:S(2)}) %copy-start.4) | copy-done | bytes 16777240
  206.1 5.2 %forward_visit.9 = (bf16[48,4096]{1,0:T(8,128)(2,1)}, bf16[3,4,48,4096]{3,2,1,0:T(8,128)(2,1)S(1)}, f32[3,4,48,256]{3,2,1,0:T(8,128)S(1)}) custom-call(s32[4]{0:T(128)S(1)} %get-tuple-element.50.info, bf16[2,48,4096]{2,1,0:T(8,128)(2,1)S(1)} %constant_dynamic-slice_fusion.feed, ...), custom_call_target="tpu_custom_call", output_to_operand_aliasing={{1}: (4, {}), {2}: (5, {})} | custom-call | flops 805306368 | bytes 16777216 | tf_op jit(solution)/shard_map/forward_visit/pallas_call | solution.py:190
  213.5 5.8 %copy-done.5 = bf16[32,2,2,256,256]{4,3,2,1,0:T(8,128)(2,1)S(1)} copy-done((bf16[32,2,2,256,256]{4,3,2,1,0:T(8,128)(2,1)S(1)}, bf16[32,2,2,256,256]{4,3,2,1,0:T(8,128)(2,1)}, u32[]{:S(2)}) %copy-start.5) | copy-done | bytes 16777240
  221.6 4.9 backward_visit.6
  230.0 14.0 %collective-permute-done.6.incoming = bf16[48,4096]{1,0:T(8,128)(2,1)} collective-permute-done((bf16[48,4096]{1,0:T(8,128)(2,1)}, bf16[48,4096]{1,0:T(8,128)(2,1)}, u32[]{:S(2)}, u32[]{:S(2)}) %collective-permute-start.6) | collective-permute-done | bytes 393248 | tf_op jit(solution)/shard_map/ppermute | solution.py:346
  244.1 5.8 %copy-done.6 = bf16[32,2,2,256,256]{4,3,2,1,0:T(8,128)(2,1)S(1)} copy-done((bf16[32,2,2,256,256]{4,3,2,1,0:T(8,128)(2,1)S(1)}, bf16[32,2,2,256,256]{4,3,2,1,0:T(8,128)(2,1)}, u32[]{:S(2)}) %copy-start.6) | copy-done | bytes 16777240
  254.5 4.9 backward_visit.7
  263.1 23.2 %collective-permute-done.7.incoming = bf16[48,4096]{1,0:T(8,128)(2,1)} collective-permute-done((bf16[48,4096]{1,0:T(8,128)(2,1)}, bf16[48,4096]{1,0:T(8,128)(2,1)}, u32[]{:S(2)}, u32[]{:S(2)}) %collective-permute-start.7) | collective-permute-done | bytes 393248 | tf_op jit(solution)/shard_map/ppermute | solution.py:346
  286.4 5.8 %copy-done.7 = bf16[32,2,2,256,256]{4,3,2,1,0:T(8,128)(2,1)S(1)} copy-done((bf16[32,2,2,256,256]{4,3,2,1,0:T(8,128)(2,1)S(1)}, bf16[32,2,2,256,256]{4,3,2,1,0:T(8,128)(2,1)}, u32[]{:S(2)}) %copy-start.7) | copy-done | bytes 16777240
  296.8 12.2 %backward_visit.8 = (bf16[48,4096]{1,0:T(8,128)(2,1)}, bf16[3,4,48,4096]{3,2,1,0:T(8,128)(2,1)S(1)}, bf16[3,4,48,256]{3,2,1,0:T(8,128)(2,1)S(1)}, bf16[3,4,48,256]{3,2,1,0:T(8,128)(2,1)S(1)}) custom-call(s32[4]{0:T(128)S(1)} %add_add_fusion.7.info, bf16[2,48,4096]{2,1,0:T(8,128)(2,1)S(1)} %copy-done.27, ...), custom_call_target="tpu_custom_call", output_to_operand_aliasing={{1}: (6, {}), {2}: (7, {}), {3}: (8, {})} | custom-call | flops 805306368 | bytes 16777216 | tf_op jit(solution)/shard_map/backward_visit/pallas_call | solution.py:225
  312.6 19.6 %collective-permute-done.8.incoming = bf16[48,4096]{1,0:T(8,128)(2,1)} collective-permute-done((bf16[48,4096]{1,0:T(8,128)(2,1)}, bf16[48,4096]{1,0:T(8,128)(2,1)}, u32[]{:S(2)}, u32[]{:S(2)}) %collective-permute-start.8) | collective-permute-done | bytes 393248 | tf_op jit(solution)/shard_map/ppermute | solution.py:346
  332.2 5.8 %copy-done.8 = bf16[32,2,2,256,256]{4,3,2,1,0:T(8,128)(2,1)S(1)} copy-done((bf16[32,2,2,256,256]{4,3,2,1,0:T(8,128)(2,1)S(1)}, bf16[32,2,2,256,256]{4,3,2,1,0:T(8,128)(2,1)}, u32[]{:S(2)}) %copy-start.8) | copy-done | bytes 16777240
  342.6 12.1 %backward_visit.9 = (bf16[48,4096]{1,0:T(8,128)(2,1)}, bf16[3,4,48,4096]{3,2,1,0:T(8,128)(2,1)S(1)}, bf16[3,4,48,256]{3,2,1,0:T(8,128)(2,1)S(1)}, bf16[3,4,48,256]{3,2,1,0:T(8,128)(2,1)S(1)}) custom-call(s32[4]{0:T(128)S(1)} %add_add_fusion.info, bf16[2,48,4096]{2,1,0:T(8,128)(2,1)S(1)} %copy-done.27, ...), custom_call_target="tpu_custom_call", output_to_operand_aliasing={{1}: (6, {}), {2}: (7, {}), {3}: (8, {})} | custom-call | flops 805306368 | bytes 16777216 | tf_op jit(solution)/shard_map/backward_visit/pallas_call | solution.py:225
  357.1 13.8 %weight_grads.1 = bf16[2,16,2,2,256,256]{5,4,3,2,1,0:T(8,128)(2,1)} custom-call(s32[4]{0:T(128)S(1)} %add_add_fusion.info, bf16[3,4,48,4096]{3,2,1,0:T(8,128)(2,1)S(1)} %copy-done.16, bf16[3,4,48,4096]{3,2,1,0:T(8,128)(2,1)S(1)} %get-tuple-element.70.kept_u, bf16[3,4,48,256]{3,2,1,0:T(8,128)(2,1)S(1)} %get-tuple-element.71.kept_h, ...), custom_call_target="tpu_custom_call" | custom-call | tf_op jit(solution)/shard_map/weight_grads/pallas_call | solution.py:271
  370.9 112.1 %reduce-scatter.2.cloned.1.call-done = bf16[1,2,2,256,256]{4,3,2,1,0:T(8,128)(2,1)} async-done(((bf16[32,2,2,256,256]{4,3,2,1,0:T(8,128)(2,1)}), bf16[1,2,2,256,256]{4,3,2,1,0:T(8,128)(2,1)}) %reduce-scatter.2.cloned.1.call-update) | async-done | bytes 524304 | tf_op jit(solution)/shard_map/reduce_scatter | solution.py:350
  485.8 5.3 %collective-permute-done.9 = bf16[2,256,256]{2,1,0:T(8,128)(2,1)S(1)} collective-permute-done((bf16[2,256,256]{2,1,0:T(8,128)(2,1)S(1)}, bf16[2,256,256]{2,1,0:T(8,128)(2,1)S(1)}, u32[]{:S(2)}, u32[]{:S(2)}) %collective-permute-start.9) | collective-permute-done | bytes 262176 | tf_op jit(solution)/shard_map/ppermute | solution.py:352
  (91 shorter events, 51.2 us)
Async XLA Ops:
  7.2 12.5 %copy-start = (bf16[4,48,4096]{2,1,0:T(8,128)(2,1)S(1)}, bf16[4,48,4096]{2,1,0:T(8,128)(2,1)}, u32[]{:S(2)}) copy-start(bf16[4,48,4096]{2,1,0:T(8,128)(2,1)} %param.5) | copy-start | bytes 4718596
  7.2 86.9 %all-gather.2.cloned.1.call-start = ((), (), s32[]{:S(2)}) async-start(), calls=%async_computation.1 | async-start | bytes 17301504 | tf_op jit(solution)/shard_map/all_gather | solution.py:303
  10.1 8.4 %collective-permute-start = (bf16[2,256,256]{2,1,0:T(8,128)(2,1)S(1)}, bf16[2,256,256]{2,1,0:T(8,128)(2,1)S(1)}, u32[]{:S(2)}, u32[]{:S(2)}) collective-permute-start(bf16[2,256,256]{2,1,0:T(8,128)(2,1)S(1)} %get-tuple-element.79), channel_id=1, source_target_pairs={{0,32},{32,0},{64,96},{96,64},{1,33},{33,1},{65,97},{97,65},{2,34}... | collective-permute-start | bytes 786440 | tf_op jit(solution)/shard_map/ppermute | solution.py:301
  19.4 463.7 %reduce-scatter.2.cloned.1.call-start = ((), (), s32[]{:S(2)}) async-start(), calls=%async_computation.2 | async-start | bytes 17301504 | tf_op jit(solution)/shard_map/reduce_scatter | solution.py:350
  94.8 5.8 %copy-start.1 = (bf16[32,2,2,256,256]{4,3,2,1,0:T(8,128)(2,1)S(1)}, bf16[32,2,2,256,256]{4,3,2,1,0:T(8,128)(2,1)}, u32[]{:S(2)}) copy-start(bf16[32,2,2,256,256]{4,3,2,1,0:T(8,128)(2,1)} %all-gather.2.cloned.1.call-done) | copy-start | bytes 50331652
  110.6 10.4 %collective-permute-start.1 = (bf16[48,4096]{1,0:T(8,128)(2,1)S(1)}, bf16[48,4096]{1,0:T(8,128)(2,1)S(1)}, u32[]{:S(2)}, u32[]{:S(2)}) collective-permute-start(bf16[48,4096]{1,0:T(8,128)(2,1)S(1)} %get-tuple-element.38), channel_id=1, source_target_pairs={{0,96},{96,64},{64,32},{1,97},{97,65},{65,33},{2,98},{98,66},{66,3... | collective-permute-start | bytes 1179656 | tf_op jit(solution)/shard_map/ppermute | solution.py:339
  121.0 5.8 %copy-start.2 = (bf16[32,2,2,256,256]{4,3,2,1,0:T(8,128)(2,1)S(1)}, bf16[32,2,2,256,256]{4,3,2,1,0:T(8,128)(2,1)}, u32[]{:S(2)}) copy-start(bf16[32,2,2,256,256]{4,3,2,1,0:T(8,128)(2,1)} %all-gather.2.cloned.1.call-done) | copy-start | bytes 50331652
  126.8 15.8 %copy-start.29 = (bf16[4,48,4096]{2,1,0:T(8,128)(2,1)S(1)}, bf16[4,48,4096]{2,1,0:T(8,128)(2,1)}, u32[]{:S(2)}) copy-start(bf16[4,48,4096]{2,1,0:T(8,128)(2,1)} %param.6) | copy-start | bytes 4718596
  136.9 13.9 %collective-permute-start.2 = (bf16[48,4096]{1,0:T(8,128)(2,1)S(1)}, bf16[48,4096]{1,0:T(8,128)(2,1)S(1)}, u32[]{:S(2)}, u32[]{:S(2)}) collective-permute-start(bf16[48,4096]{1,0:T(8,128)(2,1)S(1)} %get-tuple-element.41), channel_id=1, source_target_pairs={{0,96},{96,64},{64,32},{1,97},{97,65},{65,33},{2,98},{98,66},{66,3... | collective-permute-start | bytes 1179656 | tf_op jit(solution)/shard_map/ppermute | solution.py:339
  142.6 42.2 %copy-start.25 = (bf16[2,48,4096]{2,1,0:T(8,128)(2,1)}, bf16[2,48,4096]{2,1,0:T(8,128)(2,1)S(1)}, u32[]{:S(2)}) copy-start(bf16[2,48,4096]{2,1,0:T(8,128)(2,1)S(1)} %constant_dynamic-slice_fusion.1.feed) | copy-start | bytes 2359300
  154.0 20.0 %collective-permute-start.3 = (bf16[48,4096]{1,0:T(8,128)(2,1)S(1)}, bf16[48,4096]{1,0:T(8,128)(2,1)S(1)}, u32[]{:S(2)}, u32[]{:S(2)}) collective-permute-start(bf16[48,4096]{1,0:T(8,128)(2,1)S(1)} %get-tuple-element.44), channel_id=1, source_target_pairs={{0,96},{96,64},{64,32},{1,97},{97,65},{65,33},{2,98},{98,66},{66,3... | collective-permute-start | bytes 1179656 | tf_op jit(solution)/shard_map/ppermute | solution.py:339
  177.8 16.6 %copy-start.9 = (bf16[3,4,48,4096]{3,2,1,0:T(8,128)(2,1)}, bf16[3,4,48,4096]{3,2,1,0:T(8,128)(2,1)S(1)}, u32[]{:S(2)}) copy-start(bf16[3,4,48,4096]{3,2,1,0:T(8,128)(2,1)S(1)} %get-tuple-element.47.kept_x._) | copy-start | bytes 14155780
  177.8 20.2 %collective-permute-start.4 = (bf16[48,4096]{1,0:T(8,128)(2,1)}, bf16[48,4096]{1,0:T(8,128)(2,1)}, u32[]{:S(2)}, u32[]{:S(2)}) collective-permute-start(bf16[48,4096]{1,0:T(8,128)(2,1)} %get-tuple-element.51), channel_id=1, source_target_pairs={{0,96},{96,64},{64,32},{1,97},{97,65},{65,33},{2,98},{98,66},{66,3... | collective-permute-start | bytes 1179656 | tf_op jit(solution)/shard_map/ppermute | solution.py:339
  184.8 5.8 %copy-start.3 = (bf16[32,2,2,256,256]{4,3,2,1,0:T(8,128)(2,1)S(1)}, bf16[32,2,2,256,256]{4,3,2,1,0:T(8,128)(2,1)}, u32[]{:S(2)}) copy-start(bf16[32,2,2,256,256]{4,3,2,1,0:T(8,128)(2,1)} %all-gather.2.cloned.1.call-done) | copy-start | bytes 50331652
  196.6 16.8 %collective-permute-start.5 = (bf16[48,4096]{1,0:T(8,128)(2,1)}, bf16[48,4096]{1,0:T(8,128)(2,1)}, u32[]{:S(2)}, u32[]{:S(2)}) collective-permute-start(bf16[48,4096]{1,0:T(8,128)(2,1)} %get-tuple-element.53), channel_id=1, source_target_pairs={{96,0},{64,96},{32,64},{97,1},{65,97},{33,65},{98,2},{66,98},{34,6... | collective-permute-start | bytes 1179656 | tf_op jit(solution)/shard_map/ppermute | solution.py:346
  198.0 5.8 %copy-start.4 = (bf16[32,2,2,256,256]{4,3,2,1,0:T(8,128)(2,1)S(1)}, bf16[32,2,2,256,256]{4,3,2,1,0:T(8,128)(2,1)}, u32[]{:S(2)}) copy-start(bf16[32,2,2,256,256]{4,3,2,1,0:T(8,128)(2,1)} %all-gather.2.cloned.1.call-done) | copy-start | bytes 50331652
  203.8 2.3 copy-start.10
  206.1 7.4 %copy-start.18 = (bf16[3,4,48,4096]{3,2,1,0:T(8,128)(2,1)S(1)}, bf16[3,4,48,4096]{3,2,1,0:T(8,128)(2,1)}, u32[]{:S(2)}) copy-start(bf16[3,4,48,4096]{3,2,1,0:T(8,128)(2,1)} %copy-done.17) | copy-start | bytes 14155780
  206.1 7.4 %copy-start.26 = (bf16[2,48,4096]{2,1,0:T(8,128)(2,1)S(1)}, bf16[2,48,4096]{2,1,0:T(8,128)(2,1)}, u32[]{:S(2)}) copy-start(bf16[2,48,4096]{2,1,0:T(8,128)(2,1)} %copy-done.25) | copy-start | bytes 2359300
  213.5 5.8 %copy-start.5 = (bf16[32,2,2,256,256]{4,3,2,1,0:T(8,128)(2,1)S(1)}, bf16[32,2,2,256,256]{4,3,2,1,0:T(8,128)(2,1)}, u32[]{:S(2)}) copy-start(bf16[32,2,2,256,256]{4,3,2,1,0:T(8,128)(2,1)} %all-gather.2.cloned.1.call-done) | copy-start | bytes 50331652
  219.2 2.3 copy-start.12
  221.6 22.5 %copy-start.27 = (bf16[2,48,4096]{2,1,0:T(8,128)(2,1)S(1)}, bf16[2,48,4096]{2,1,0:T(8,128)(2,1)}, u32[]{:S(2)}) copy-start(bf16[2,48,4096]{2,1,0:T(8,128)(2,1)} %copy-done.25) | copy-start | bytes 2359300
  228.7 15.4 %collective-permute-start.6 = (bf16[48,4096]{1,0:T(8,128)(2,1)}, bf16[48,4096]{1,0:T(8,128)(2,1)}, u32[]{:S(2)}, u32[]{:S(2)}) collective-permute-start(bf16[48,4096]{1,0:T(8,128)(2,1)} %get-tuple-element.58), channel_id=1, source_target_pairs={{96,0},{64,96},{32,64},{97,1},{65,97},{33,65},{98,2},{66,98},{34,6... | collective-permute-start | bytes 1179656 | tf_op jit(solution)/shard_map/ppermute | solution.py:346
  244.1 5.8 %copy-start.6 = (bf16[32,2,2,256,256]{4,3,2,1,0:T(8,128)(2,1)S(1)}, bf16[32,2,2,256,256]{4,3,2,1,0:T(8,128)(2,1)}, u32[]{:S(2)}) copy-start(bf16[32,2,2,256,256]{4,3,2,1,0:T(8,128)(2,1)} %all-gather.2.cloned.1.call-done) | copy-start | bytes 50331652
  249.8 2.3 copy-start.13
  252.2 2.3 copy-start.20
  261.6 24.8 %collective-permute-start.7 = (bf16[48,4096]{1,0:T(8,128)(2,1)}, bf16[48,4096]{1,0:T(8,128)(2,1)}, u32[]{:S(2)}, u32[]{:S(2)}) collective-permute-start(bf16[48,4096]{1,0:T(8,128)(2,1)} %get-tuple-element.62), channel_id=1, source_target_pairs={{96,0},{64,96},{32,64},{97,1},{65,97},{33,65},{98,2},{66,98},{34,6... | collective-permute-start | bytes 1179656 | tf_op jit(solution)/shard_map/ppermute | solution.py:346
  286.4 5.8 %copy-start.7 = (bf16[32,2,2,256,256]{4,3,2,1,0:T(8,128)(2,1)S(1)}, bf16[32,2,2,256,256]{4,3,2,1,0:T(8,128)(2,1)}, u32[]{:S(2)}) copy-start(bf16[32,2,2,256,256]{4,3,2,1,0:T(8,128)(2,1)} %all-gather.2.cloned.1.call-done) | copy-start | bytes 50331652
  311.2 21.0 %collective-permute-start.8 = (bf16[48,4096]{1,0:T(8,128)(2,1)}, bf16[48,4096]{1,0:T(8,128)(2,1)}, u32[]{:S(2)}, u32[]{:S(2)}) collective-permute-start(bf16[48,4096]{1,0:T(8,128)(2,1)} %get-tuple-element.66), channel_id=1, source_target_pairs={{96,0},{64,96},{32,64},{97,1},{65,97},{33,65},{98,2},{66,98},{34,6... | collective-permute-start | bytes 1179656 | tf_op jit(solution)/shard_map/ppermute | solution.py:346
  332.2 5.8 %copy-start.8 = (bf16[32,2,2,256,256]{4,3,2,1,0:T(8,128)(2,1)S(1)}, bf16[32,2,2,256,256]{4,3,2,1,0:T(8,128)(2,1)}, u32[]{:S(2)}) copy-start(bf16[32,2,2,256,256]{4,3,2,1,0:T(8,128)(2,1)} %all-gather.2.cloned.1.call-done) | copy-start | bytes 50331652
  370.9 120.3 %copy-start.28 = (bf16[2,1,256,256]{3,2,1,0:T(8,128)(2,1)S(1)}, bf16[2,1,256,256]{3,2,1,0:T(8,128)(2,1)}, u32[]{:S(2)}) copy-start(bf16[2,1,256,256]{3,2,1,0:T(8,128)(2,1)} %param.7) | copy-start | bytes 786436
  484.1 7.0 %collective-permute-start.9 = (bf16[2,256,256]{2,1,0:T(8,128)(2,1)S(1)}, bf16[2,256,256]{2,1,0:T(8,128)(2,1)S(1)}, u32[]{:S(2)}, u32[]{:S(2)}) collective-permute-start(bf16[2,256,256]{2,1,0:T(8,128)(2,1)S(1)} %get-tuple-element.77), channel_id=1, source_target_pairs={{0,32},{32,0},{64,96},{96,64},{1,33},{33,1},{65,97},{97,65},{2,34}... | collective-permute-start | bytes 786440 | tf_op jit(solution)/shard_map/ppermute | solution.py:352
  (10 other events, 22.5 us)
Sparse Core Ops, SparseCore 0:
  19.5 74.5 all-gather.1
  371.1 111.9 reduce-scatter.1
